TPU v7x, 128 devices: a whole 4x4x4 slice. The times are simulated.
128 devices in a mesh: lon: 8 (over x, y_hi), dp: 16 (over z, y_lo, core).
Axes of the slice: x: 4, y: 4 (y_hi: 2, y_lo: 2; y = y_hi * 2 + y_lo), z: 4, core: 2. Of those that a mesh axis runs over, the one named last changes fastest.
Arguments:
- latents: bfloat16 [16, 16, 512, 640], P('dp', None, 'lon'), may hold values from -24 to 24
- target: bfloat16 [16, 16, 512, 640], P('dp', None, 'lon'), may hold values from -14 to 14
- norm_gain: float32 [640], replicated, may hold values from 0.25 to 1.75
- norm_shift: float32 [640], replicated, may hold values from -3 to 3
- conv_weight: bfloat16 [640, 3, 3, 640], P('dp'), may hold values from -0.078125 to 0.078125
- conv_bias: float32 [640], replicated, may hold values from -2 to 2
- timesteps: int32 [16], P('dp'), may hold values from 0 to 999
- buckets: int32 [16], P('dp'), may hold values from 0 to 3
- clip_milli: int32 [4], replicated, may hold values from 1000 to 11999
Outputs:
- bucket_losses: float32 [4], replicated
- input_grad: bfloat16 [16, 16, 512, 640], P('dp', None, 'lon')
- weight_grad: float32 [640, 3, 3, 640], P('dp')
- gain_grad: float32 [640], replicated
- shift_grad: float32 [640], replicated
- bias_grad: float32 [640], replicated
All inputs are finite; a program needn't handle non-finite values.
Results may differ from a plain program's by a relative error of at most 0.015.
Values may be sent and summed in bfloat16 or wider, within the bound.
A program may use at most 448 MiB of HBM per device.

v0:
```python
import jax
import jax.numpy as jnp
from jax import lax
from jax.sharding import PartitionSpec as P

GROUPS = 32
NB = 4


def with_halo(value, sides, width):
    for axis, dim in sides:
        size, length = (lax.axis_size(axis), value.shape[dim])
        up = [(i, (i + 1) % size) for i in range(size)]
        down = [(j, i) for i, j in up]
        last = lax.slice_in_dim(value, length - width, length, axis=dim)
        leading = lax.slice_in_dim(value, 0, width, axis=dim)
        before = lax.ppermute(last, axis, up)
        after = lax.ppermute(leading, axis, down)
        value = jnp.concatenate([before, value, after], axis=dim)
    return value


def circular(field):
    wide = with_halo(field, (("lon", 2),), 1)
    return jnp.pad(wide, ((0, 0), (1, 1), (0, 0), (0, 0)))


def grouped(per_chan):
    pans = per_chan.shape[0]
    return jnp.sum(per_chan.reshape(pans, GROUPS, -1), axis=2)


def spread(stat, chans):
    return jnp.repeat(stat, chans // GROUPS, axis=1)[:, None, None, :]


def stacked_taps(padded, amount, rows, cols):
    pixels = padded.shape[0] * rows * cols
    listed = []
    for kh in range(3):
        for kw in range(3):
            listed.append(padded[:, kh : kh + rows, kw : kw + cols, :].reshape(pixels, amount))
    return jnp.concatenate(listed, axis=1)


def tap_products(padded, amount, rows, cols, grad_flat):
    stacked = stacked_taps(padded, amount, rows, cols)
    result = lax.dot_general(
        stacked, grad_flat, (((0,), (0,)), ((), ())), preferred_element_type=jnp.float32
    )
    return jnp.transpose(result.reshape(3, 3, amount, grad_flat.shape[1]), (2, 0, 1, 3))


def shards(
    latents, target, norm_gain, norm_shift, conv_weight, conv_bias, timesteps, buckets, clip_milli
):
    lon_count = lax.axis_size("lon")
    pans, rows, cols, chans = latents.shape
    pixels = pans * rows * cols
    count = rows * cols * lon_count * (chans // GROUPS)
    field = latents.astype(jnp.float32)
    chan_sum = jnp.sum(field, axis=(1, 2))
    mean = lax.psum(grouped(chan_sum), "lon") / count
    centered = field - spread(mean, chans)
    var = lax.psum(grouped(jnp.sum(centered * centered, axis=(1, 2))), "lon") / count
    rstd = lax.rsqrt(var + 1e-05)
    normed = centered * spread(rstd, chans)
    pre = normed * norm_gain + norm_shift
    act = jax.nn.silu(pre).astype(jnp.bfloat16)
    act_pad = circular(act)
    piece = lax.all_gather(conv_weight, "dp", axis=0, tiled=True)
    width = piece.shape[0]
    stacked = stacked_taps(act_pad, width, rows, cols)
    flat_weight = jnp.transpose(piece, (1, 2, 0, 3)).reshape(9 * width, chans)
    forward = jnp.dot(stacked, flat_weight, preferred_element_type=jnp.float32)
    branch = forward.reshape(pans, rows, cols, chans) + conv_bias
    err = field + branch - target.astype(jnp.float32)
    tweight = 1.0 / (1.0 + timesteps.astype(jnp.float32) / 250.0)
    pano_part = tweight * jnp.sum(err * err, axis=(1, 2, 3)) / (rows * cols * lon_count * chans)
    member = (buckets[:, None] == jnp.arange(NB, dtype=jnp.int32)[None, :]).astype(jnp.float32)
    totals, counts = lax.psum(
        (jnp.sum(member * pano_part[:, None], axis=0), jnp.sum(member, axis=0) / lon_count),
        ("lon", "dp"),
    )
    denom = jnp.maximum(counts, 1.0)
    bucket_mean = totals / denom
    limit = clip_milli.astype(jnp.float32) / 1000.0
    bucket_losses = jnp.minimum(bucket_mean, limit)
    passing = (bucket_mean < limit).astype(jnp.float32)
    coef = tweight * jnp.sum(member * (passing / denom)[None, :], axis=1)
    grad_out = (coef[:, None, None, None] * err).astype(jnp.bfloat16)
    grad_pad = circular(grad_out)
    piece = lax.all_gather(conv_weight, "dp", axis=0, tiled=True)
    result = jnp.zeros((pixels, piece.shape[0]), jnp.float32)
    for kh in range(3):
        for kw in range(3):
            tap = grad_pad[:, kh : kh + rows, kw : kw + cols, :].reshape(pixels, chans)
            result = result + lax.dot_general(
                tap,
                piece[:, 2 - kh, 2 - kw, :],
                (((1,), (1,)), ((), ())),
                preferred_element_type=jnp.float32,
            )
    dact = result
    dact = dact.reshape(pans, rows, cols, chans)
    sig = jax.nn.sigmoid(pre)
    dpre = dact * sig * (1.0 + pre * (1.0 - sig))
    dnorm = dpre * norm_gain
    first_back, second_back = lax.psum(
        (grouped(jnp.sum(dnorm, axis=(1, 2))), grouped(jnp.sum(dnorm * normed, axis=(1, 2)))), "lon"
    )
    dfield = spread(rstd, chans) * (
        dnorm - spread(first_back / count, chans) - normed * spread(second_back / count, chans)
    )
    input_grad = (grad_out.astype(jnp.float32) + dfield).astype(jnp.bfloat16)
    scale = 1.0 / (rows * cols)
    gain_sum, shift_sum, bias_sum = lax.psum(
        (
            jnp.sum(dpre * normed, axis=(0, 1, 2)),
            jnp.sum(dpre, axis=(0, 1, 2)),
            jnp.sum(grad_out.astype(jnp.float32), axis=(0, 1, 2)),
        ),
        ("lon", "dp"),
    )
    dp_rows = chans // lax.axis_size("dp")
    flat_grad = grad_out.reshape(pixels, chans)
    local_rows = lax.psum_scatter(
        tap_products(act_pad, dp_rows * lax.axis_size("dp"), rows, cols, flat_grad).astype(
            jnp.bfloat16
        ),
        "dp",
        scatter_dimension=0,
        tiled=True,
    )
    weight_grad = lax.psum(local_rows, "lon").astype(jnp.float32) * scale
    return (
        bucket_losses,
        input_grad,
        weight_grad,
        gain_sum * scale,
        shift_sum * scale,
        bias_sum * scale,
    )


def solution(mesh):
    placed = (
        P("dp", None, "lon", None),
        P("dp", None, "lon", None),
        P(),
        P(),
        P("dp", None, None, None),
        P(),
        P("dp"),
        P("dp"),
        P(),
    )
    return jax.shard_map(
        shards,
        mesh=mesh,
        in_specs=placed,
        out_specs=(P(), P("dp", None, "lon", None), P("dp", None, None, None), P(), P(), P()),
        check_vma=False,
    )
```

profile of v0, /device:TPU:1, one launch (start us, length us, event | category | flops | bytes accessed | tf_op | source)
XLA Modules:
  0.0 473.3 jit_solution(8566913652491641244)
XLA Ops:
  8.0 1.6 convert_reduce_fusion
  9.8 21.6 %psum.70 = f32[1,32]{1,0:T(1,128)S(1)} all-reduce(f32[1,32]{1,0:T(1,128)S(1)} %bitcast.140), channel_id=1, replica_groups=mesh['lon'=8,'dp'=16] {'lon'}, use_global_device_ids=true, to_apply=%region_2.0 | all-reduce | flops 32 | bytes 256 | tf_op jit(solution)/shard_map/psum | solution.py:63
  32.2 15.9 %psum.71 = f32[1,32]{1,0:T(1,128)S(1)} all-reduce(f32[1,32]{1,0:T(1,128)S(1)} %bitcast.141), channel_id=1, replica_groups=mesh['lon'=8,'dp'=16] {'lon'}, use_global_device_ids=true, to_apply=%region_5.0 | all-reduce | flops 32 | bytes 256 | tf_op jit(solution)/shard_map/psum | solution.py:65
  48.3 0.9 fusion.14
  49.3 3.2 collective-permute-start.1
  54.2 0.8 collective-permute-done.1
  54.9 4.5 collective-permute-done
  60.1 1.7 fusion.38
  61.8 1.2 constant_dynamic-update-slice_fusion.8
  63.0 1.2 constant_dynamic-update-slice_fusion.7
  64.3 1.2 constant_dynamic-update-slice_fusion.6
  67.4 1.2 constant_dynamic-update-slice_fusion.5
  68.6 1.2 constant_dynamic-update-slice_fusion.4
  69.8 1.0 bitcast_dynamic-update-slice_fusion.4
  71.5 1.3 constant_dynamic-update-slice_fusion.3
  72.8 1.7 constant_dynamic-update-slice_fusion.2
  74.6 2.1 constant_dynamic-update-slice_fusion.1
  76.7 1.3 constant_dynamic-update-slice_fusion
  77.9 16.3 %copy.17 = bf16[5760,1024]{1,0:T(8,128)(2,1)} copy(bf16[5760,1024]{0,1:T(8,128)(2,1)} %bitcast.54) | data formatting | bytes 23592960 | tf_op jit(solution)/shard_map/dot_general | solution.py:48
  94.2 1.3 bitcast_dynamic-update-slice_fusion.2
  95.5 1.5 bitcast_dynamic-update-slice_fusion.1
  97.1 1.6 bitcast_dynamic-update-slice_fusion
  98.7 16.4 %multiply_reduce_fusion = (f32[]{:T(128)}, f32[1,16,64,640]{3,2,1,0:T(8,128)}) fusion(bf16[1,16,64,640]{3,2,1,0:T(8,128)(2,1)} %param.10, f32[640]{0:T(1024)S(1)} %copy-done.5, bf16[16,64,5760]{2,1,0:T(8,128)(2,1)} %bitcast_dynamic-update-slice_fusion, bf16[5760,640,1]{1,0,2:T(8,128)(2,1)} %bitcast.135, bf16[1,16,64,640]{3,2,1,0:T(8,128)(2,1)S(1)} %copy-done), kind=kOutput, calls=%fused_computation.34 | convolution fusion | flops 7554334720 | bytes 24414724 | tf_op jit(solution)/shard_map/dot_general | solution.py:75
  115.7 73.0 %all-reduce.4 = (f32[4]{0:T(128)S(1)}, f32[4]{0:T(128)S(1)}) all-reduce(f32[4]{0:T(128)S(1)} %get-tuple-element.47, f32[4]{0:T(128)S(1)} %get-tuple-element.46), channel_id=1, replica_groups=mesh['lon'=8,'dp'=16] {'lon','dp'}, use_global_device_ids=true, to_apply=%region_7.8 | all-reduce | flops 8 | bytes 64 | tf_op jit(solution)/shard_map/psum | solution.py:81
  190.0 2.2 convert_reduce_fusion.1
  192.2 15.3 %convert_bitcast_fusion = bf16[640,3,3,640]{3,0,2,1:T(8,128)(2,1)} fusion(bf16[3,3,640,1024]{3,2,1,0:T(8,128)(2,1)} %bitcast.118, bf16[1024,640,1,1]{1,0,3,2:T(8,128)(2,1)S(1)} %bitcast.116), kind=kOutput, calls=%fused_computation | convolution fusion | flops 7553433600 | bytes 20480000 | tf_op jit(solution)/shard_map/dot_general | solution.py:48
  209.5 2.8 collective-permute-start.3
  212.5 2.5 fusion.28
  215.5 3.4 collective-permute-done.2
  218.9 0.8 pad_maximum_fusion
  220.4 1.9 fusion.39
  222.3 0.8 slice-done.1
  223.1 1.3 fusion.25
  224.4 1.3 fusion.26
  225.8 1.3 fusion.27
  227.1 1.3 fusion.29
  228.5 1.3 fusion.30
  229.8 2.5 fusion.32
  232.3 2.5 fusion.31
  234.8 2.9 add_add_fusion
  237.7 2.9 fusion.20
  241.0 17.6 %all-reduce.5 = (f32[1,32]{1,0:T(1,128)S(1)}, f32[1,32]{1,0:T(1,128)S(1)}) all-reduce(f32[1,32]{1,0:T(1,128)S(1)} %bitcast.138, f32[1,32]{1,0:T(1,128)S(1)} %bitcast.139), channel_id=1, replica_groups=mesh['lon'=8,'dp'=16] {'lon'}, use_global_device_ids=true, to_apply=%region_15.16 | all-reduce | flops 64 | bytes 512 | tf_op jit(solution)/shard_map/psum | solution.py:109
  258.6 68.5 %all-reduce.3 = (f32[640]{0:T(1024)S(1)}, f32[640]{0:T(1024)S(1)}, f32[640]{0:T(1024)S(1)}) all-reduce(f32[640]{0:T(1024)S(1)} %get-tuple-element.6, f32[640]{0:T(1024)S(1)} %get-tuple-element.9, f32[640]{0:T(1024)S(1)} %get-tuple-element.17), channel_id=1, replica_groups=mesh['lon'=8,'dp'=16] {'lon','dp'}, use_global_device_ids=true, to_apply=%region_19.20 | all-reduce | flops 1920 | bytes 15360 | tf_op jit(solution)/shard_map/psum | solution.py:117
  328.9 51.8 %all-reduce.11.cloned.1.call-done = bf16[640,3,3,640]{3,0,2,1:T(8,128)(2,1)} async-done(((bf16[640,3,3,640]{3,0,2,1:T(8,128)(2,1)}), bf16[640,3,3,640]{3,0,2,1:T(8,128)(2,1)}) %all-reduce.11.cloned.1.call-update) | async-done | bytes 7372816
  380.7 1.8 constant_dynamic-slice_fusion
  382.9 3.7 fusion.22
  386.6 77.9 %all-reduce.9.cloned.1.call-done = bf16[40,3,3,640]{3,0,2,1:T(8,128)(2,1)} async-done(((bf16[40,3,3,640]{3,0,2,1:T(8,128)(2,1)}), bf16[40,3,3,640]{3,0,2,1:T(8,128)(2,1)}) %all-reduce.9.cloned.1.call-update) | async-done | bytes 460816 | tf_op jit(solution)/shard_map/psum | solution.py:135
  464.5 2.0 convert_multiply_fusion
  (65 shorter events, 11.6 us)
Async XLA Ops:
  7.2 24.4 %copy-start = (bf16[1,16,64,640]{3,2,1,0:T(8,128)(2,1)S(1)}, bf16[1,16,64,640]{3,2,1,0:T(8,128)(2,1)}, u32[]{:S(2)}) copy-start(bf16[1,16,64,640]{3,2,1,0:T(8,128)(2,1)} %param.9) | copy-start | bytes 3932164
  7.2 41.1 %copy-start.3 = (f32[640]{0:T(1024)S(1)}, f32[640]{0:T(1024)}, u32[]{:S(2)}) copy-start(f32[640]{0:T(1024)} %param.12) | copy-start | bytes 7684
  7.2 41.1 %copy-start.2 = (f32[640]{0:T(1024)S(1)}, f32[640]{0:T(1024)}, u32[]{:S(2)}) copy-start(f32[640]{0:T(1024)} %param.11) | copy-start | bytes 7684
  7.2 91.5 %all-gather.2.cloned.1.call-start = ((), (), s32[]{:S(2)}) async-start(), calls=%async_computation | async-start | bytes 7833600 | tf_op jit(solution)/shard_map/all_gather | solution.py:71
  7.9 372.8 %all-reduce.11.cloned.1.call-start = ((), (), s32[]{:S(2)}) async-start(), calls=%async_computation.2 | async-start | bytes 14745600
  49.3 5.6 %collective-permute-start.1 = (bf16[1,16,1,640]{3,2,1,0:T(2,128)(2,1)S(1)}, bf16[1,16,1,640]{3,2,1,0:T(2,128)(2,1)S(1)}, u32[]{:S(2)}, u32[]{:S(2)}) collective-permute-start(bf16[1,16,1,640]{3,2,1,0:T(2,128)(2,1)S(1)} %get-tuple-element.43), channel_id=1, source_target_pairs={{16,0},{32,16},{48,32},{64,48},{80,64},{96,80},{112,96},{0,112},{1... | collective-permute-start | bytes 61448 | tf_op jit(solution)/shard_map/ppermute | solution.py:18
  52.5 6.8 %collective-permute-start = (bf16[1,16,1,640]{3,2,1,0:T(2,128)(2,1)S(1)}, bf16[1,16,1,640]{3,2,1,0:T(2,128)(2,1)S(1)}, u32[]{:S(2)}, u32[]{:S(2)}) collective-permute-start(bf16[1,16,1,640]{3,2,1,0:T(2,128)(2,1)S(1)} %get-tuple-element.42), channel_id=1, source_target_pairs={{0,16},{16,32},{32,48},{48,64},{64,80},{80,96},{96,112},{112,0},{1... | collective-permute-start | bytes 61448 | tf_op jit(solution)/shard_map/ppermute | solution.py:17
  71.5 6.4 %copy-start.1 = (bf16[16,64,5760]{2,1,0:T(8,128)(2,1)}, bf16[16,64,5760]{2,1,0:T(8,128)(2,1)S(1)}, u32[]{:S(2)}) copy-start(bf16[16,64,5760]{2,1,0:T(8,128)(2,1)S(1)} %get-tuple-element.22) | copy-start | bytes 35389444
  95.5 3.2 copy-start.5
  98.7 90.1 %copy-start.4 = (s32[4]{0:T(128)S(1)}, s32[4]{0:T(128)}, u32[]{:S(2)}) copy-start(s32[4]{0:T(128)} %param.17) | copy-start | bytes 52
  207.5 0.7 copy-start.6
  207.6 257.0 %all-reduce.9.cloned.1.call-start = ((), (), s32[]{:S(2)}) async-start(), calls=%async_computation.1 | async-start | bytes 921600 | tf_op jit(solution)/shard_map/psum | solution.py:135
  209.5 6.0 %collective-permute-start.3 = (bf16[1,16,1,640]{3,2,1,0:T(2,128)(2,1)S(1)}, bf16[1,16,1,640]{3,2,1,0:T(2,128)(2,1)S(1)}, u32[]{:S(2)}, u32[]{:S(2)}) collective-permute-start(bf16[1,16,1,640]{3,2,1,0:T(2,128)(2,1)S(1)} %get-tuple-element.41), channel_id=1, source_target_pairs={{16,0},{32,16},{48,32},{64,48},{80,64},{96,80},{112,96},{0,112},{1... | collective-permute-start | bytes 61448 | tf_op jit(solution)/shard_map/ppermute | solution.py:18
  212.3 6.6 %collective-permute-start.2 = (bf16[1,16,1,640]{3,2,1,0:T(2,128)(2,1)S(1)}, bf16[1,16,1,640]{3,2,1,0:T(2,128)(2,1)S(1)}, u32[]{:S(2)}, u32[]{:S(2)}) collective-permute-start(bf16[1,16,1,640]{3,2,1,0:T(2,128)(2,1)S(1)} %get-tuple-element.40), channel_id=1, source_target_pairs={{0,16},{16,32},{32,48},{48,64},{64,80},{80,96},{96,112},{112,0},{1... | collective-permute-start | bytes 61448 | tf_op jit(solution)/shard_map/ppermute | solution.py:17
  219.7 2.6 slice-start
  220.4 2.7 slice-start.1
Sparse Core Ops, SparseCore 0:
  9.7 52.6 all-gather.1
  207.7 172.9 all-reduce.10
  383.8 80.6 all-reduce.8
where the time goes:
time: 481 us; the launch traced here: 473 us
  blocking collectives  197 us (41%)
  waiting for transfers between devices  139 us (29%)
  matrix products  48.7 us (10%)
  local copies, waits for them, and re-layouts  43.1 us (9%)
  other arithmetic  21.6 us (4%)
  between operations  17.6 us (4%)
  starting transfers between devices  6.67 us (1%)
    psum x1, waiting for transfers between devices, shards(): weight_grad = lax.psum(local_rows, 'lon').astype(jnp.float32) * scale  77.9 us
    psum x1, blocking collectives, shards(): lax.psum((jnp.sum(member * pano_part[:, None], axis=0), jnp.sum(member, a...  73 us
    psum x1, blocking collectives, shards(): lax.psum((jnp.sum(dpre * normed, axis=(0, 1, 2)), jnp.sum(dpre, axis=(0,...  68.5 us
    unnamed x4, waiting for transfers between devices  52.5 us
    psum x1, blocking collectives, shards(): mean = lax.psum(grouped(chan_sum), 'lon') / count  21.6 us
    unnamed x33, local copies, waits for them, and re-layouts  19.2 us
    psum x1, blocking collectives, shards(): lax.psum((grouped(jnp.sum(dnorm, axis=(1, 2))), grouped(jnp.sum(dnorm * n...  17.6 us
    dot_general x9, matrix products, shards(): lax.dot_general(tap, piece[:, 2 - kh, 2 - kw, :], (((1,), (1,)), ((), ())...  17 us
  transfers between devices with their start and end apart: 7, of which 5 were waited for; matrix products, arithmetic and copies ran while one was open for 16% of the time, Pallas kernels for 0%

commit v1 on v0

v1 whole, which is shorter than its diff:
```python
import functools

import jax
import jax.numpy as jnp
from jax import lax
from jax.experimental import pallas as pl
from jax.experimental.pallas import tpu as pltpu
from jax.sharding import PartitionSpec as P

F32 = jnp.float32
BF16 = jnp.bfloat16
ROWS, COLS, C = 16, 64, 640
PIX = ROWS * COLS
PADPIX = PIX + 2 * COLS
NLON, NDP = 8, 16
COUNT = ROWS * COLS * NLON * (C // 32)
SCALE = 1.0 / (ROWS * COLS)
ORDERS = ("xyz", "yzx", "zxy")
LANES = ((0, 256), (256, 512), (512, 640))
NT = (((1,), (1,)), ((), ()))


class Sems:
    def __init__(self):
        self.used = 0

    def take(self, n=1):
        first = self.used
        self.used += n
        return first


NUM_SEMS = 200


def kernel(
    ts, bk, clip, lat_in, tgt_in, win_in, gain_r, shift_r, bias_r,
    igrad, wout, sg_out,
    lat, tgt, win, dsilu, sibw, wg_all, x3, x3t, acc, dacc, e3, agb,
    mask, stat, hs, hr, es, er, l1, l2, g1, g2, sem, *red,
):
    lon, dp = lax.axis_index("lon"), lax.axis_index("dp")
    x, yhi = lon // 2, lon % 2
    z, ylo, c = dp // 4, (dp // 2) % 2, dp % 2
    y = yhi * 2 + ylo
    here = {"x": x, "y": y, "z": z}
    alloc = Sems()

    def dev(xx, yy, zz, cc):
        return {"lon": xx * 2 + yy // 2, "dp": (zz * 2 + yy % 2) * 2 + cc}

    def along(axis, step):
        at = dict(here)
        at[axis] = (at[axis] + step) % 4
        return dev(at["x"], at["y"], at["z"], c)

    sibling = dev(x, y, z, 1 - c)

    def rcopy(src, dst, send, recv, to):
        return pltpu.make_async_remote_copy(
            src_ref=src, dst_ref=dst, send_sem=sem.at[send], recv_sem=sem.at[recv],
            device_id=to, device_id_type=pl.DeviceIdType.MESH,
        )

    def got(ref, number):
        rcopy(ref, ref, number, number, sibling).wait_recv()

    def sent(ref, number):
        rcopy(ref, ref, number, number, sibling).wait_send()

    def to_lon(i):
        return {"lon": i, "dp": dp}

    def to_dp(i):
        return {"lon": lon, "dp": i}

    loads = [
        pltpu.make_async_copy(src, dst, sem.at[alloc.take()])
        for src, dst in ((win_in, win), (lat_in, lat), (tgt_in, tgt))
    ]
    for one in loads:
        one.start()

    bar = pltpu.get_barrier_semaphore()

    def greet(to):
        pl.semaphore_signal(bar, inc=1, device_id=to, device_id_type=pl.DeviceIdType.MESH)

    @pl.loop(1, NLON)
    def _(k):
        greet(to_lon((lon + k) % NLON))

    @pl.loop(1, NDP)
    def _(k):
        greet(to_dp((dp + k) % NDP))

    far = (y + 3 + 2 * ylo) % 4
    greet(dev(x, far, z, c))

    class Exchange:
        def __init__(self, rx, me, size, to):
            self.rx, self.me, self.size, self.to = rx, me, size, to
            self.base = alloc.take(2)

        def send(self):
            @pl.loop(1, self.size)
            def _(k):
                slot = self.rx.at[self.me]
                rcopy(slot, slot, self.base, self.base + 1, self.to((self.me + k) % self.size)).start()

        def wait(self):
            others = self.rx.at[0 : self.size - 1]
            sent(others, self.base)
            got(others, self.base + 1)

        def total(self):
            return functools.reduce(lambda a, b: a + b, [self.rx[i] for i in range(self.size)])

    def at_row(r):
        return pl.ds(pl.multiple_of(r * COLS, COLS), COLS)

    def sums(r, tot):
        v = lat[r].astype(F32)
        hs[0, pl.ds(r, 1), :] = v[COLS - 1 : COLS]
        hs[1, pl.ds(r, 1), :] = v[0:1]
        return tot + jnp.sum(v, axis=0, keepdims=True)

    loads[1].wait()
    chan = lax.fori_loop(0, ROWS, sums, jnp.zeros((1, C), F32))
    gi = jnp.floor((lax.broadcasted_iota(jnp.int32, (C, C), 0).astype(F32) + 0.5) * 0.05)
    gj = jnp.floor((lax.broadcasted_iota(jnp.int32, (C, C), 1).astype(F32) + 0.5) * 0.05)
    mask[...] = jnp.where(gi == gj, 1.0, 0.0).astype(BF16)

    def group_sum(v):
        top = v.astype(BF16)
        rest = v - top.astype(F32)
        mid = rest.astype(BF16)
        low = (rest - mid.astype(F32)).astype(BF16)
        zeros = jnp.zeros((8, C), F32)
        terms = jnp.concatenate(
            [top.astype(F32), mid.astype(F32), low.astype(F32), zeros], axis=0
        ).astype(BF16)
        out = jnp.dot(terms, mask[...], preferred_element_type=F32)
        return out[0:8] + out[8:16] + out[16:24]

    sub = lax.broadcasted_iota(jnp.int32, (8, C), 0)
    pl.semaphore_wait(bar, NLON - 1 + NDP - 1 + 1)
    loads[0].wait()

    swaps = alloc.take(6)

    def swap_tap(j):
        return rcopy(win.at[2 * j + 1 - c], sibw.at[j], swaps, swaps + 1 + j, sibling)

    for j in range(4):
        swap_tap(j).start()
    pl.when(c == 1)(lambda: swap_tap(4).start())

    right, left = to_lon((lon + 1) % NLON), to_lon((lon + NLON - 1) % NLON)
    hsem = alloc.take(2)
    rcopy(hs.at[0], hr.at[0], hsem, hsem + 1, right).start()
    rcopy(hs.at[1], hr.at[1], hsem, hsem + 1, left).start()

    local_mean = group_sum(jnp.where(sub == 0, chan, 0.0))[0:1] / (PIX * 20)

    odd = x % 2
    own_d = z * 2 + ylo

    def jyz(slot, core):
        return (odd, 2 + (1 - core) * odd, 4 - core)[slot]

    def jx(slot):
        return (1 - odd, 3 - odd)[slot]

    def assemble(j):
        got(sibw.at[j], swaps + 1 + j)
        a = win[2 * j + c].astype(F32)
        b = sibw[j].astype(F32)
        first = jnp.where(c == 0, a, b)
        second = jnp.where(c == 0, b, a)
        rows = pl.ds(pl.multiple_of(own_d * 80, 16), 80)
        wg_all[2 * j + c, rows, :] = jnp.concatenate([first, second], axis=0).astype(BF16)

    LO, HI = (0, 48), (48, 32)

    def blk(j, zz, parity, part=(0, 80)):
        row = pl.multiple_of((zz * 2 + parity) * 80 + part[0], 16)
        return wg_all.at[2 * j + c, pl.ds(row, part[1]), :]

    zl, zr, zo = (z + 3) % 4, (z + 1) % 4, (z + 2) % 4
    gz = [alloc.take(3) for _ in range(3)]
    gy = [alloc.take(5) for _ in range(3)]
    gx = [alloc.take(8) for _ in range(2)]
    gd = [alloc.take(2) for _ in range(5)]

    def rows_of(n):
        return wg_all.at[0, 0:n]

    def two_ways(axis, j, zz, parity, send, recv, slot):
        plus, minus = (LO, HI) if slot % 2 == 0 else (HI, LO)
        one, two = blk(j, zz, parity, plus), blk(j, zz, parity, minus)
        return (
            rcopy(one, one, send, recv, along(axis, 1)),
            rcopy(two, two, send, recv, along(axis, 3)),
        )

    def y_copies(s, k, zz):
        return two_ways("y", jyz(s, c), zz, ylo, gy[s], gy[s] + 1 + k, s)

    def x_copies(s, k, zz, parity):
        return two_ways("x", jyz(s, c), zz, parity, gx[s], gx[s] + k, s)

    def z1(s):
        block = blk(jyz(s, c), z, ylo)
        return [rcopy(block, block, gz[s], gz[s] + 1, along("z", k)) for k in (1, 3)]

    def z2(s):
        j = jyz(s, c)
        plus, minus = (LO, HI) if s % 2 == 0 else (HI, LO)
        one, two = blk(j, zl, ylo, plus), blk(j, zr, ylo, minus)
        return (
            rcopy(one, one, gz[s], gz[s] + 2, along("z", 1)),
            rcopy(two, two, gz[s], gz[s] + 2, along("z", 3)),
        )

    def start(copies):
        for one in copies:
            one.start()

    AROUND = (z, zl, zr, zo)

    def over_x(s, body):
        if s == 0:
            body()
        elif s == 1:
            pl.when(c == 0)(body)

    BLOCKS = ((z, ylo), (zl, ylo), (zr, ylo), (zo, ylo), *((q, 1 - ylo) for q in AROUND))

    def across(n, j, core, k):
        zz, parity = BLOCKS[k]
        row = pl.multiple_of((zz * 2 + parity) * 80, 16)
        block = wg_all.at[2 * j + core, pl.ds(row, 80), :]
        return rcopy(block, block, gd[n], gd[n] + 1, sibling)

    def give(n, j, ks):
        start([across(n, j, c, k) for k in ks])

    def wave1(s):
        assemble(jyz(s, c))
        start(z1(s))
        start(y_copies(s, 0, z))
        give(s, jyz(s, c), (0,))

    def x_send(s, ks):
        def body():
            for k in ks:
                start(x_copies(s, k, *BLOCKS[k]))

        over_x(s, body)

    def wave2(s):
        got(rows_of(160), gz[s] + 1)
        start(z2(s))
        start(y_copies(s, 1, zl))
        start(y_copies(s, 2, zr))
        x_send(s, (1, 2))
        give(s, jyz(s, c), (1, 2))

    def wave3(s):
        got(rows_of(80), gz[s] + 2)
        start(y_copies(s, 3, zo))
        x_send(s, (3,))
        give(s, jyz(s, c), (3,))

    def wave4(s):
        for k in range(4):
            got(rows_of(80), gy[s] + 1 + k)
            x_send(s, (4 + k,))
            give(s, jyz(s, c), (4 + k,))

    def own_x(s):
        def body():
            assemble(jx(s))
            give(3 + s, jx(s), (0,))

        over_x(s, body)

    def wave_x(s, ks):
        def body():
            for k in ks:
                got(rows_of(80), gx[s] + k)
                give(3 + s, jx(s), (k,))

        over_x(s, body)

    def from_sibling(s):
        got(rows_of(C), gd[s] + 1)

    def from_sibling_x(s):
        def body():
            got(rows_of(C), gd[3 + s] + 1)

        if s == 0:
            body()
        else:
            pl.when(c == 1)(body)

    def sends_done():
        pl.when(c == 0)(lambda: sent(sibw.at[0:4], swaps))
        pl.when(c == 1)(lambda: sent(sibw, swaps))
        for s in range(3):
            sent(rows_of(240), gz[s])
            sent(rows_of(320), gy[s])
            sent(rows_of(C), gd[s])
        for s in range(2):

            def body(s=s):
                sent(rows_of(560), gx[s])
                sent(rows_of(C), gd[3 + s])

            over_x(s, body)

    wave1(0)
    wave1(1)
    dacc[...] = jnp.zeros((PIX + 4 * COLS, C), F32)
    own_x(0)
    own_x(1)

    def squares(r, tot):
        d = lat[r].astype(F32) - local_mean
        return tot + jnp.sum(d * d, axis=0, keepdims=True)

    chan2 = lax.fori_loop(0, ROWS, squares, jnp.zeros((1, C), F32))
    m2loc = group_sum(jnp.where(sub == 0, chan2, 0.0))[0:1]
    stat[lon] = jnp.where(sub == 0, local_mean, jnp.where(sub == 1, m2loc, 0.0))
    ex_stat = Exchange(stat, lon, NLON, to_lon)
    ex_stat.send()

    wave2(0)
    wave1(2)
    ex_stat.wait()
    sent(hs, hsem)
    got(hr, hsem + 1)
    stats = [stat[i] for i in range(NLON)]
    mean = functools.reduce(lambda a, b: a + b, [s[0:1] for s in stats]) / NLON
    spread = functools.reduce(lambda a, b: a + b, [(s[0:1] - mean) * (s[0:1] - mean) for s in stats])
    within = functools.reduce(lambda a, b: a + b, [s[1:2] for s in stats])
    var = (within + (PIX * 20) * spread) / COUNT
    rstd = lax.rsqrt(var + 1e-05)
    gain, shift = gain_r[...].reshape(1, C), shift_r[...].reshape(1, C)

    def pre_of(v):
        normed = (v - mean) * rstd
        return normed, normed * gain + shift

    def silu(v):
        _, pre = pre_of(v)
        return pre * jax.nn.sigmoid(pre)

    hr[0] = silu(hr[0])
    hr[1] = silu(hr[1])
    edge = lax.broadcasted_iota(jnp.int32, (COLS, C), 0)

    def put_sides(dst, to, a, halo, r):
        before = jnp.where(edge == 0, halo[0, pl.ds(r, 1), :], pltpu.roll(a, 1, 0))
        after = jnp.where(edge == COLS - 1, halo[1, pl.ds(r, 1), :], pltpu.roll(a, COLS - 1, 0))
        dst[at_row(to), 0:C] = before.astype(BF16)
        dst[at_row(to), 2 * C : 3 * C] = after.astype(BF16)

    zero_row = jnp.zeros((COLS, 3 * C), BF16)
    for buf, ends in ((x3, (0, PADPIX - COLS)), (e3, (0, COLS, PADPIX, PADPIX + COLS))):
        for low in ends:
            buf[low : low + COLS, :] = zero_row

    def activate(first, end):
        @pl.loop(first, end)
        def _(r):
            _normed, pre = pre_of(lat[r].astype(F32))
            sig = jax.nn.sigmoid(pre)
            a = pre * sig
            dsilu[r] = sig * (1.0 + pre * (1.0 - sig))
            x3[at_row(r + 1), C : 2 * C] = a.astype(BF16)
            put_sides(x3, r + 1, a, hr, r)

    unit = jnp.where(
        lax.broadcasted_iota(jnp.int32, (256, 256), 0) == lax.broadcasted_iota(jnp.int32, (256, 256), 1),
        1.0, 0.0,
    ).astype(BF16)

    def turn(first, end):
        for j in range(first, end):
            low, high = j * 256, min(j * 256 + 256, 3 * C)
            n = high - low
            x3t[low:high, :] = lax.dot_general(
                unit[:n, :n], x3[:, low:high], NT, preferred_element_type=F32
            ).astype(BF16)

    def forward(tap, count, fresh=False):
        @pl.loop(0, 2)
        def _(m):
            fields = []
            for n in range(count):
                kh, kw = (tap + n) // 3, (tap + n) % 3
                rows = pl.ds(pl.multiple_of(kh * COLS + m * 512, COLS), 512)
                fields.append(x3[rows, pl.ds(pl.multiple_of(kw * C, 128), C)])
            w = wg_all[pl.ds(tap, count)].reshape(count * C, C)
            part = jnp.dot(jnp.concatenate(fields, axis=1), w, preferred_element_type=F32)
            out = pl.ds(pl.multiple_of(m * 512, 512), 512)
            acc[out, :] = part if fresh else acc[out, :] + part

    activate(0, 8)
    wave2(1)
    wave3(0)
    activate(8, ROWS)
    wave3(1)
    wave4(0)
    wave_x(0, (1, 2))
    turn(0, 3)
    wave2(2)
    wave_x(0, (3,))
    from_sibling(0)
    forward(2 * odd, 2, True)
    wave4(1)
    wave_x(1, (1, 2, 3))
    wave3(2)
    wave_x(0, (4, 5, 6, 7))
    turn(3, 8)
    from_sibling_x(0)
    forward(2 - 2 * odd, 2)
    wave_x(1, (4, 5, 6, 7))
    wave4(2)
    from_sibling(1)
    from_sibling_x(1)
    forward(4, 3)
    from_sibling(2)
    forward(7, 2)
    sends_done()

    loads[2].wait()
    bias = bias_r[...].reshape(1, C)

    def error(r, carry):
        sq, tot = carry
        v = acc[at_row(r), :] + bias + lat[r].astype(F32) - tgt[r].astype(F32)
        e3[at_row(r + 2), C : 2 * C] = v.astype(BF16)
        es[0, pl.ds(r, 1), :] = v[COLS - 1 : COLS]
        es[1, pl.ds(r, 1), :] = v[0:1]
        return sq + jnp.sum(v * v, axis=0, keepdims=True), tot + jnp.sum(v, axis=0, keepdims=True)

    zero = jnp.zeros((1, C), F32)
    sq, err_sum = lax.fori_loop(0, ROWS, error, (zero, zero))
    l1[lon] = jnp.broadcast_to(jnp.sum(sq, axis=1, keepdims=True), (8, 128))
    ex_l1 = Exchange(l1, lon, NLON, to_lon)
    ex_l1.send()
    esem = alloc.take(2)
    rcopy(es.at[0], er.at[0], esem, esem + 1, right).start()
    rcopy(es.at[1], er.at[1], esem, esem + 1, left).start()

    def back(m):
        low = m * (PADPIX // 3)
        w = jnp.concatenate(
            [
                jnp.concatenate([wg_all[3 * kh + kw] for kw in (2, 1, 0)], axis=1)
                for kh in range(3)
            ],
            axis=0,
        )
        part = lax.dot_general(
            e3[COLS + low : COLS + low + PADPIX // 3, :], w, NT, preferred_element_type=F32
        )
        for kh in range(3):
            out = slice(low + kh * COLS, low + kh * COLS + PADPIX // 3)
            dacc[out, :] = dacc[out, :] + part[:, kh * C : (kh + 1) * C]

    NRED = 9
    groups = [red[NRED * g : NRED * g + NRED] for g in range(3)]

    def order(kw, g):
        return ORDERS[(kw + g) % 3]

    def place(kw, g, core, lon_to, d):
        at = {"x": lon_to // 2, "y": (lon_to % 2) * 2 + d % 2, "z": d // 2}
        a1, a2, a3 = order(kw, g)
        return kw, core, at[a1], at[a2], at[a3]

    def weight_part(kw):
        for g in range(3):
            first, end = LANES[g]
            for d in range(8):
                groups[g][0][place(kw, g, 1, 7, d)] = jnp.zeros((16, end - first), BF16)
        err = jnp.concatenate(
            [e3[(2 - kh) * COLS : (2 - kh) * COLS + PADPIX, C : 2 * C] for kh in range(3)], axis=1
        )
        for half in range(2):
            top = kw * C + half * (C // 2)
            res = jnp.dot(x3t[top : top + C // 2, :], err, preferred_element_type=F32)
            res = res.astype(BF16)
            for d in range(4):
                for t in range(5):
                    low = d * 80 + t * 16
                    for kh in range(3):
                        s = kh * 5 + t
                        for g in range(3):
                            first, end = LANES[g]
                            groups[g][0][place(kw, g, s % 2, s // 2, half * 4 + d)] = res[
                                low : low + 16, kh * C + first : kh * C + end
                            ]

    def add(out, terms):
        val = functools.reduce(lambda a, b: a + b, [t[...].astype(F32) for t in terms])
        out[...] = val.astype(out.dtype)

    send_sems = [alloc.take(4) for _ in range(3)]

    def reduce_sends_done():
        for g in range(3):
            rxs, r2rx, r3 = groups[g][1], groups[g][7], groups[g][8]
            sent(rxs, send_sems[g])
            sent(rxs.at[:, 0:3], send_sems[g] + 1)
            sent(r2rx, send_sems[g] + 2)
            sent(r3.at[:, 4:7], send_sems[g] + 3)

    class Lanes:
        def __init__(self, kw, g):
            wg, rxs, ra, rb, rc, rd, r2, r2rx, r3 = groups[g]
            self.r3rx = r3.at[kw, 4:7]
            self.kw, self.g, self.axes = kw, g, order(kw, g)
            self.rxs, self.r2, self.r2rx, self.r3 = rxs.at[kw], r2.at[kw], r2rx.at[kw], r3.at[kw]
            self.ra, self.rb, self.rc, self.rd = ra.at[kw], rb.at[kw], rc.at[kw], rd.at[kw]
            self.buf = wg.at[kw, c]
            send, self.recv = send_sems[g], alloc.take(5)
            self.two = wg.at[kw, 0, 0:2]
            self.swap = rcopy(wg.at[kw, 1 - c], self.rxs, send, self.recv, sibling)
            axis = self.axes[0]
            self.me = [here[a] for a in self.axes]
            far_, up, down = ((self.me[0] + k) % 4 for k in (2, 1, 3))
            self.up, self.down = up, down
            self.first = [
                rcopy(src, dst, send + 1, self.recv + n, along(axis, to))
                for src, dst, n, to in (
                    (self.buf.at[far_, 0:2], self.ra, 1, 1),
                    (self.buf.at[far_, 2:4], self.rb, 1, 3),
                    (self.buf.at[up], self.rc, 2, 1),
                    (self.buf.at[down], self.rd, 2, 3),
                )
            ]
            self.second = self.direct(1, self.r2, self.r2rx, send + 2, self.recv + 3)
            self.third = self.direct(2, self.r3, self.r3rx, send + 3, self.recv + 4)

        def direct(self, stage, buf, rx, send, recv):
            return [
                rcopy(
                    buf.at[(self.me[stage] + k) % 4], rx.at[k - 1],
                    send, recv, along(self.axes[stage], k),
                )
                for k in (1, 3, 2)
            ]

        def join(self, mine_by, theirs_by):
            got(self.rxs, self.recv)

            @pl.loop(0, 4)
            def _(i):
                own = self.buf[i].astype(F32) * mine_by
                self.buf[i] = (own + self.rxs[i].astype(F32) * theirs_by).astype(BF16)

            start(self.first[:2])

        def middle(self):
            got(self.rc, self.recv + 1)
            add(self.buf.at[self.up, 0:2], [self.buf.at[self.up, 0:2], self.ra])
            add(self.buf.at[self.down, 2:4], [self.buf.at[self.down, 2:4], self.rb])
            start(self.first[2:])

        def end_first(self):
            got(self.two, self.recv + 2)
            add(self.r2, [self.buf.at[self.me[0]], self.rc, self.rd])
            start(self.second)

        def end_second(self):
            got(self.r2rx, self.recv + 3)
            add(self.r3.at[0:4], [self.r2.at[self.me[1]]] + [self.r2rx.at[k] for k in range(3)])
            start(self.third)

        def end_third(self):
            got(self.r3rx, self.recv + 4)
            val = self.r3[self.me[2]].astype(F32)
            for k in range(3):
                val = val + self.r3[4 + k].astype(F32)
            first, end = LANES[self.g]
            agb[self.kw, c, lon, :, first:end] = val.astype(BF16)

    class Reduce:
        def __init__(self, kw):
            self.kw = kw
            self.lanes = [Lanes(kw, g) for g in range(3)]
            slot = agb.at[kw, c, lon]
            self.sems = alloc.take(5)
            send, recv = self.sems, self.sems + 1
            self.over_y = rcopy(slot, slot, send, recv, dev(x, (y + 2) % 4, z, c))
            pair = agb.at[kw, c, pl.ds(2 * x, 2)]
            self.over_x = [rcopy(pair, pair, send, recv + 1, along("x", k)) for k in (1, 3, 2)]
            self.give = rcopy(agb.at[kw, c], agb.at[kw, c], send + 3, recv + 3, sibling)

        def join(self, mine_by, theirs_by):
            for one in self.lanes:
                one.join(mine_by, theirs_by)

        def step(self, n):
            kw = self.kw
            if n == 0:
                for one in self.lanes:
                    one.swap.start()
            elif n == 2:
                for one in self.lanes:
                    one.middle()
            elif n == 3:
                for one in self.lanes:
                    one.end_first()
            elif n == 4:
                for one in self.lanes:
                    one.end_second()
            elif n == 5:
                for one in self.lanes:
                    one.end_third()
                self.over_y.start()
            elif n == 6:
                got(agb.at[kw, c, 0], self.sems + 1)
                start(self.over_x)
            elif n == 7:
                got(agb.at[kw, c, 0:6], self.sems + 2)
                self.give.start()
            elif n == 8:
                got(agb.at[kw, 1 - c], self.sems + 4)
                sent(agb.at[kw, c, 0:7], self.sems)
                sent(agb.at[kw, c], self.sems + 3)
                for row in range(3):
                    tiles = []
                    for t in range(5):
                        s = row * 5 + t
                        tiles.append(agb[kw, s % 2, s // 2].astype(F32))
                    rows = jnp.concatenate(tiles, axis=0)
                    wout[3 * row + kw] = jnp.where(c == 0, rows[0:40], rows[40:80]) * SCALE

    parts = [Reduce(kw) for kw in range(3)]
    weight_part(0)
    parts[0].step(0)

    ex_l1.wait()
    tweight = 1.0 / (1.0 + jnp.full((8, 128), ts[0], jnp.int32).astype(F32) / 250.0)
    pano = tweight * ex_l1.total() / (ROWS * COLS * NLON * C)
    lane = lax.broadcasted_iota(jnp.int32, (8, 128), 1)
    row8 = lax.broadcasted_iota(jnp.int32, (8, 128), 0)
    member = jnp.where(lane == jnp.full((8, 128), bk[0], jnp.int32), 1.0, 0.0).astype(F32)
    l2[dp] = jnp.where(
        row8 == 0, member * pano, jnp.where(row8 == 1, member, jnp.where(row8 == 2, tweight, 0.0))
    )
    ex_l2 = Exchange(l2, dp, NDP, to_dp)
    ex_l2.send()
    weight_part(1)
    parts[1].step(0)
    ex_l2.wait()
    sums2 = ex_l2.total()
    denom = jnp.maximum(sums2[1:2], 1.0)
    bucket_mean = sums2[0:1] / denom
    lane1 = lane[0:1]
    limit = jnp.zeros((1, 128), jnp.int32)
    for b in range(4):
        limit = jnp.where(lane1 == b, jnp.full((1, 128), clip[b], jnp.int32), limit)
    limit = limit.astype(F32) / 1000.0
    losses = jnp.minimum(bucket_mean, limit)
    passing = jnp.where((bucket_mean < limit) & (lane1 < 4), 1.0, 0.0)

    def coef_of(tile):
        picked = jnp.sum(tile[1:2] * passing / denom, axis=1, keepdims=True)
        return tile[2:3, 0:1] * picked

    coef, sib_coef = coef_of(l2[dp]), coef_of(l2[dp + 1 - 2 * c])

    parts[0].join(coef, sib_coef)
    weight_part(2)
    parts[2].step(0)
    parts[1].join(coef, sib_coef)
    parts[0].step(2)

    sent(es, esem)
    got(er, esem + 1)

    @pl.loop(0, ROWS)
    def _(r):
        put_sides(e3, r + 2, e3[at_row(r + 2), C : 2 * C].astype(F32), er, r)

    parts[1].step(2)
    parts[2].join(coef, sib_coef)
    parts[0].step(3)
    back(0)
    parts[2].step(2)
    parts[1].step(3)
    parts[0].step(4)
    back(1)
    parts[2].step(3)
    parts[1].step(4)
    parts[0].step(5)
    back(2)
    parts[2].step(4)
    parts[1].step(5)
    parts[0].step(6)

    def through(r, carry):
        a, b = carry
        normed = (lat[r].astype(F32) - mean) * rstd
        dpre = dacc[at_row(r + 2), :] * coef * dsilu[r]
        dacc[at_row(r + 2), :] = dpre
        return (
            a + jnp.sum(dpre, axis=0, keepdims=True),
            b + jnp.sum(dpre * normed, axis=0, keepdims=True),
        )

    s1, s2 = lax.fori_loop(0, ROWS, through, (zero, zero))
    g1[lon] = jnp.where(
        sub == 0, s1, jnp.where(sub == 1, s2, jnp.where(sub == 2, err_sum * coef, 0.0))
    )
    ex_g1 = Exchange(g1, lon, NLON, to_lon)
    ex_g1.send()
    parts[2].step(5)
    parts[1].step(6)
    parts[0].step(7)
    ex_g1.wait()
    pan = ex_g1.total()
    g2[dp] = pan
    ex_g2 = Exchange(g2, dp, NDP, to_dp)
    ex_g2.send()
    means = group_sum(pan * gain) / COUNT
    m1, m2 = means[0:1], means[1:2]

    @pl.loop(0, ROWS)
    def _(r):
        normed = (lat[r].astype(F32) - mean) * rstd
        dn = dacc[at_row(r + 2), :] * gain
        g = e3[at_row(r + 2), C : 2 * C].astype(F32) * coef
        igrad[r] = (g + rstd * (dn - m1 - normed * m2)).astype(BF16)

    parts[2].step(6)
    parts[1].step(7)
    parts[0].step(8)
    ex_g2.wait()
    totals = ex_g2.total() * SCALE
    wide = jnp.concatenate([losses] + [jnp.zeros_like(losses)] * 4, axis=1)
    sg_out[...] = jnp.where(sub == 3, wide, totals)
    parts[2].step(7)
    parts[1].step(8)
    parts[2].step(8)
    reduce_sends_done()
    assert alloc.used <= NUM_SEMS, alloc.used


def reduce_shapes(lanes):
    tile = (16, lanes)
    return [
        (3, 2, 4, 4, 4, *tile),
        (3, 4, 4, 4, *tile),
        (3, 2, 4, *tile),
        (3, 2, 4, *tile),
        (3, 4, 4, *tile),
        (3, 4, 4, *tile),
        (3, 4, 4, *tile),
        (3, 3, 4, *tile),
        (3, 7, *tile),
    ]


def shards(
    latents, target, norm_gain, norm_shift, conv_weight, conv_bias, timesteps, buckets, clip_milli
):
    win = jnp.transpose(conv_weight, (1, 2, 0, 3)).reshape(9, 40, C)
    vmem = pl.BlockSpec(memory_space=pltpu.VMEM)
    smem = pl.BlockSpec(memory_space=pltpu.SMEM)
    outs = pl.pallas_call(
        kernel,
        out_shape=(
            pltpu.VMEM((ROWS, COLS, C), BF16),
            pltpu.VMEM((9, 40, C), F32),
            pltpu.VMEM((8, C), F32),
        ),
        in_specs=[smem] * 3 + [pl.BlockSpec(memory_space=pl.ANY)] * 3 + [vmem] * 3,
        out_specs=(vmem,) * 3,
        scratch_shapes=[
            pltpu.VMEM((ROWS, COLS, C), BF16),
            pltpu.VMEM((ROWS, COLS, C), BF16),
            pltpu.VMEM((9, 40, C), BF16),
            pltpu.VMEM((ROWS, COLS, C), F32),
            pltpu.VMEM((5, 40, C), BF16),
            pltpu.VMEM((9, C, C), BF16),
            pltpu.VMEM((PADPIX, 3 * C), BF16),
            pltpu.VMEM((3 * C, PADPIX), BF16),
            pltpu.VMEM((PIX, C), F32),
            pltpu.VMEM((PIX + 4 * COLS, C), F32),
            pltpu.VMEM((PADPIX + 2 * COLS, 3 * C), BF16),
            pltpu.VMEM((3, 2, NLON, 16, C), BF16),
            pltpu.VMEM((C, C), BF16),
            pltpu.VMEM((NLON, 8, C), F32),
            pltpu.VMEM((2, ROWS, C), F32),
            pltpu.VMEM((2, ROWS, C), F32),
            pltpu.VMEM((2, ROWS, C), F32),
            pltpu.VMEM((2, ROWS, C), F32),
            pltpu.VMEM((NLON, 8, 128), F32),
            pltpu.VMEM((NDP, 8, 128), F32),
            pltpu.VMEM((NLON, 8, C), F32),
            pltpu.VMEM((NDP, 8, C), F32),
            pltpu.SemaphoreType.DMA((NUM_SEMS,)),
        ]
        + [pltpu.VMEM(shape, BF16) for first, end in LANES for shape in reduce_shapes(end - first)],
        compiler_params=pltpu.CompilerParams(
            collective_id=0, has_side_effects=True, vmem_limit_bytes=60 * 1024 * 1024
        ),
        cost_estimate=pl.CostEstimate(
            flops=3 * 2 * PIX * 9 * C * C, bytes_accessed=8 * 1024 * 1024, transcendentals=2 * PIX * C
        ),
    )(
        timesteps, buckets, clip_milli, latents[0], target[0], win,
        norm_gain, norm_shift, conv_bias,
    )
    igrad, wout, sg = outs
    weight_grad = jnp.transpose(wout.reshape(3, 3, 40, C), (2, 0, 1, 3))
    return sg[3, :4], igrad[None], weight_grad, sg[1], sg[0], sg[2]


def solution(mesh):
    placed = (
        P("dp", None, "lon", None),
        P("dp", None, "lon", None),
        P(),
        P(),
        P("dp", None, None, None),
        P(),
        P("dp"),
        P("dp"),
        P(),
    )
    return jax.shard_map(
        shards,
        mesh=mesh,
        in_specs=placed,
        out_specs=(P(), P("dp", None, "lon", None), P("dp", None, None, None), P(), P(), P()),
        check_vma=False,
    )
```

time: 481 us -> 98.6 us (0.20); the launches traced: 473 us -> 98.5 us
  blocking collectives: 197 us -> 0 us
  waiting for transfers between devices: 139 us -> 0 us
  Pallas kernels: 0 us -> 93.4 us
  matrix products: 48.7 us -> 0 us
  local copies, waits for them, and re-layouts: 43.1 us -> 3.11 us
  other arithmetic: 21.6 us -> 0 us
  between operations: 17.6 us -> 1.94 us
  starting transfers between devices: 6.67 us -> 0 us
    psum x5 -> x0, blocking collectives: 197 us -> none  [the longest x1 73 us: shards(): lax.psum((jnp.sum(member * pano_part[:, None], axis=0), jnp.sum(member, a...]
    pallas_call x0 -> x1, Pallas kernels: none -> 93.4 us  [shards(): pl.pallas_call(kernel, out_shape=(pltpu.VMEM((ROWS, COLS, C), BF16), pltp...]
    psum x1 -> x0, waiting for transfers between devices: 77.9 us -> none  [shards(): weight_grad = lax.psum(local_rows, 'lon').astype(jnp.float32) * scale]
    unnamed x4 -> x0, waiting for transfers between devices: 52.5 us -> none
    dot_general x11 -> x0, matrix products: 48.7 us -> none  [the longest x9 17 us: shards(): lax.dot_general(tap, piece[:, 2 - kh, 2 - kw, :], (((1,), (1,)), ((), ())...]
    unnamed x33 -> x2, local copies, waits for them, and re-layouts: 19.2 us -> 1.98 us
    dot_general x1 -> x0, local copies, waits for them, and re-layouts: 16.3 us -> none  [tap_products(): lax.dot_general(stacked, grad_flat, (((0,), (0,)), ((), ())), preferred_e...]
    ppermute x4 -> x0, waiting for transfers between devices: 8.59 us -> none  [the longest x2 7.83 us: with_halo(): before = lax.ppermute(last, axis, up)]
  transfers between devices with their start and end apart: 7 -> 0, of which waited for: 5 -> 0; matrix products, arithmetic and copies ran while one was open for 16% -> 0% of each run, Pallas kernels for 0% -> 0%
where the time goes in v1:
time: 98.6 us; the launch traced here: 98.5 us
  Pallas kernels  93.4 us (95%)
  local copies, waits for them, and re-layouts  3.11 us (3%)
  between operations  1.94 us (2%)
    pallas_call x1, Pallas kernels, shards(): pl.pallas_call(kernel, out_shape=(pltpu.VMEM((ROWS, COLS, C), BF16), pltp...  93.4 us
    unnamed x2, local copies, waits for them, and re-layouts  1.98 us

profile of v1, /device:TPU:1, one launch (start us, length us, event | category | flops | bytes accessed | tf_op | source)
XLA Modules:
  0.0 98.5 jit_solution(15810440319175676921)
XLA Ops:
  1.9 93.4 %shard_map.136 = (bf16[16,64,640]{2,1,0:T(8,128)(2,1)S(1)}, f32[9,40,640]{2,1,0:T(8,128)S(1)}, f32[8,640]{1,0:T(8,128)S(1)}) custom-call(s32[1]{0:T(128)S(6)} %copy.19.ts, s32[1]{0:T(128)S(6)} %copy.20.bk, s32[4]{0:T(128)} %clip.1, bf16[16,64,640]{2,1,0:T(8,128)(2,1)} %bitcast.13, bf16[16,64,640]{2,1,0:T(8,128)(2,1)} %bitcast.14, ...), custom_call_target="tpu_custom_call" | custom-call | flops 22649241600 | bytes 8388608 | tf_op jit(solution)/shard_map/pallas_call | solution.py:779
  95.3 0.6 slice_reduce_fusion
  96.0 0.5 slice_bitcast_fusion
  96.5 1.1 %copy.17 = bf16[1,16,64,640]{3,2,1,0:T(8,128)(2,1)} copy(bf16[1,16,64,640]{3,2,1,0:T(8,128)(2,1)S(1)} %bitcast.11) | data formatting | bytes 2621440
  97.5 0.9 copy.18

commit v2 on v1

--- a/solution.py
+++ b/solution.py
@@ -181,11 +181,9 @@
         rows = pl.ds(pl.multiple_of(own_d * 80, 16), 80)
         wg_all[2 * j + c, rows, :] = jnp.concatenate([first, second], axis=0).astype(BF16)
 
-    LO, HI = (0, 48), (48, 32)
-
-    def blk(j, zz, parity, part=(0, 80)):
-        row = pl.multiple_of((zz * 2 + parity) * 80 + part[0], 16)
-        return wg_all.at[2 * j + c, pl.ds(row, part[1]), :]
+    def blk(j, zz, parity):
+        row = pl.multiple_of((zz * 2 + parity) * 80, 16)
+        return wg_all.at[2 * j + c, pl.ds(row, 80), :]
 
     zl, zr, zo = (z + 3) % 4, (z + 1) % 4, (z + 2) % 4
     gz = [alloc.take(3) for _ in range(3)]
@@ -196,32 +194,23 @@
     def rows_of(n):
         return wg_all.at[0, 0:n]
 
-    def two_ways(axis, j, zz, parity, send, recv, slot):
-        plus, minus = (LO, HI) if slot % 2 == 0 else (HI, LO)
-        one, two = blk(j, zz, parity, plus), blk(j, zz, parity, minus)
-        return (
-            rcopy(one, one, send, recv, along(axis, 1)),
-            rcopy(two, two, send, recv, along(axis, 3)),
-        )
-
-    def y_copies(s, k, zz):
-        return two_ways("y", jyz(s, c), zz, ylo, gy[s], gy[s] + 1 + k, s)
-
-    def x_copies(s, k, zz, parity):
-        return two_ways("x", jyz(s, c), zz, parity, gx[s], gx[s] + k, s)
+    def one_way(axis, block, send, recv, up):
+        return rcopy(block, block, send, recv, along(axis, 1 if up else 3))
+
+    def y_copy(s, k, zz):
+        block = blk(jyz(s, c), zz, ylo)
+        return one_way("y", block, gy[s], gy[s] + 1 + k, (k in (0, 3)) == (s != 1))
+
+    def x_copy(s, k, zz, parity):
+        block = blk(jyz(s, c), zz, parity)
+        return one_way("x", block, gx[s], gx[s] + k, (k % 2 == 0) == (s == 0))
 
     def z1(s):
         block = blk(jyz(s, c), z, ylo)
-        return [rcopy(block, block, gz[s], gz[s] + 1, along("z", k)) for k in (1, 3)]
+        return [one_way("z", block, gz[s], gz[s] + 1, up) for up in (True, False)]
 
     def z2(s):
-        j = jyz(s, c)
-        plus, minus = (LO, HI) if s % 2 == 0 else (HI, LO)
-        one, two = blk(j, zl, ylo, plus), blk(j, zr, ylo, minus)
-        return (
-            rcopy(one, one, gz[s], gz[s] + 2, along("z", 1)),
-            rcopy(two, two, gz[s], gz[s] + 2, along("z", 3)),
-        )
+        return one_way("z", blk(jyz(s, c), zr if s == 1 else zl, ylo), gz[s], gz[s] + 2, s != 1)
 
     def start(copies):
         for one in copies:
@@ -244,32 +233,37 @@
         return rcopy(block, block, gd[n], gd[n] + 1, sibling)
 
     def give(n, j, ks):
-        start([across(n, j, c, k) for k in ks])
+        if n in (0, 1, 3):
+            if ks[-1] == 7:
+                tap = wg_all.at[2 * j + c]
+                rcopy(tap, tap, gd[n], gd[n] + 1, sibling).start()
+        else:
+            start([across(n, j, c, k) for k in ks])
 
     def wave1(s):
         assemble(jyz(s, c))
         start(z1(s))
-        start(y_copies(s, 0, z))
+        y_copy(s, 0, z).start()
         give(s, jyz(s, c), (0,))
 
     def x_send(s, ks):
         def body():
             for k in ks:
-                start(x_copies(s, k, *BLOCKS[k]))
+                x_copy(s, k, *BLOCKS[k]).start()
 
         over_x(s, body)
 
     def wave2(s):
         got(rows_of(160), gz[s] + 1)
-        start(z2(s))
-        start(y_copies(s, 1, zl))
-        start(y_copies(s, 2, zr))
+        z2(s).start()
+        y_copy(s, 1, zl).start()
+        y_copy(s, 2, zr).start()
         x_send(s, (1, 2))
         give(s, jyz(s, c), (1, 2))
 
     def wave3(s):
         got(rows_of(80), gz[s] + 2)
-        start(y_copies(s, 3, zo))
+        y_copy(s, 3, zo).start()
         x_send(s, (3,))
         give(s, jyz(s, c), (3,))
 
@@ -479,8 +473,8 @@
     def order(kw, g):
         return ORDERS[(kw + g) % 3]
 
-    def place(kw, g, core, lon_to, d):
-        at = {"x": lon_to // 2, "y": (lon_to % 2) * 2 + d % 2, "z": d // 2}
+    def place(kw, g, core, lon_to, d, z_from=0):
+        at = {"x": lon_to // 2, "y": (lon_to % 2) * 2 + d % 2, "z": z_from + d // 2}
         a1, a2, a3 = order(kw, g)
         return kw, core, at[a1], at[a2], at[a3]
 
@@ -489,12 +483,13 @@
             first, end = LANES[g]
             for d in range(8):
                 groups[g][0][place(kw, g, 1, 7, d)] = jnp.zeros((16, end - first), BF16)
-        err = jnp.concatenate(
-            [e3[(2 - kh) * COLS : (2 - kh) * COLS + PADPIX, C : 2 * C] for kh in range(3)], axis=1
-        )
-        for half in range(2):
-            top = kw * C + half * (C // 2)
-            res = jnp.dot(x3t[top : top + C // 2, :], err, preferred_element_type=F32)
+        @pl.loop(0, 2)
+        def _(half):
+            err = jnp.concatenate(
+                [e3[(2 - kh) * COLS : (2 - kh) * COLS + PADPIX, C : 2 * C] for kh in range(3)], axis=1
+            )
+            top = pl.ds(pl.multiple_of(kw * C + half * (C // 2), C // 2), C // 2)
+            res = jnp.dot(x3t[top, :], err, preferred_element_type=F32)
             res = res.astype(BF16)
             for d in range(4):
                 for t in range(5):
@@ -503,7 +498,7 @@
                         s = kh * 5 + t
                         for g in range(3):
                             first, end = LANES[g]
-                            groups[g][0][place(kw, g, s % 2, s // 2, half * 4 + d)] = res[
+                            groups[g][0][place(kw, g, s % 2, s // 2, d, 2 * half)] = res[
                                 low : low + 16, kh * C + first : kh * C + end
                             ]
 
@@ -728,9 +723,9 @@
     parts[0].step(7)
     ex_g1.wait()
     pan = ex_g1.total()
-    g2[dp] = pan
-    ex_g2 = Exchange(g2, dp, NDP, to_dp)
-    ex_g2.send()
+    g2[z] = pan
+    ex_z = Exchange(g2.at[0:4], z, 4, lambda i: dev(x, y, i, c))
+    ex_z.send()
     means = group_sum(pan * gain) / COUNT
     m1, m2 = means[0:1], means[1:2]
 
@@ -742,6 +737,10 @@
         igrad[r] = (g + rstd * (dn - m1 - normed * m2)).astype(BF16)
 
     parts[2].step(6)
+    ex_z.wait()
+    g2[4 + dp % 4] = ex_z.total()
+    ex_g2 = Exchange(g2.at[4:8], dp % 4, 4, lambda i: to_dp(z * 4 + i))
+    ex_g2.send()
     parts[1].step(7)
     parts[0].step(8)
     ex_g2.wait()
@@ -807,7 +806,7 @@
             pltpu.VMEM((NLON, 8, 128), F32),
             pltpu.VMEM((NDP, 8, 128), F32),
             pltpu.VMEM((NLON, 8, C), F32),
-            pltpu.VMEM((NDP, 8, C), F32),
+            pltpu.VMEM((8, 8, C), F32),
             pltpu.SemaphoreType.DMA((NUM_SEMS,)),
         ]
         + [pltpu.VMEM(shape, BF16) for first, end in LANES for shape in reduce_shapes(end - first)],

time: 98.6 us -> 103 us (1.045)
  Pallas kernels: 93.4 us -> 98.1 us
    pallas_call x1, Pallas kernels: 93.4 us -> 98.1 us  [shards(): pl.pallas_call(kernel, out_shape=(pltpu.VMEM((ROWS, COLS, C), BF16), pltp...]
where the time goes in v2:
time: 103 us
  Pallas kernels  98.1 us (95%)
  local copies, waits for them, and re-layouts  3.11 us (3%)
  between operations  1.94 us (2%)
    pallas_call x1, Pallas kernels, shards(): pl.pallas_call(kernel, out_shape=(pltpu.VMEM((ROWS, COLS, C), BF16), pltp...  98.1 us

profile of v2, /device:TPU:1, one launch (start us, length us, event | category | flops | bytes accessed | tf_op | source)
XLA Modules:
  0.0 103.1 jit_solution(18382586522379459576)
XLA Ops:
  1.9 98.1 %shard_map.136 = (bf16[16,64,640]{2,1,0:T(8,128)(2,1)S(1)}, f32[9,40,640]{2,1,0:T(8,128)S(1)}, f32[8,640]{1,0:T(8,128)S(1)}) custom-call(s32[1]{0:T(128)S(6)} %copy.19.ts, s32[1]{0:T(128)S(6)} %copy.20.bk, s32[4]{0:T(128)} %clip.1, bf16[16,64,640]{2,1,0:T(8,128)(2,1)} %bitcast.13, bf16[16,64,640]{2,1,0:T(8,128)(2,1)} %bitcast.14, ...), custom_call_target="tpu_custom_call" | custom-call | flops 22649241600 | bytes 8388608 | tf_op jit(solution)/shard_map/pallas_call | solution.py:778
  100.0 0.6 slice_reduce_fusion
  100.6 0.5 slice_bitcast_fusion
  101.1 1.1 %copy.17 = bf16[1,16,64,640]{3,2,1,0:T(8,128)(2,1)} copy(bf16[1,16,64,640]{3,2,1,0:T(8,128)(2,1)S(1)} %bitcast.11) | data formatting | bytes 2621440
  102.2 0.9 copy.18

commit v3 on v1

--- a/solution.py
+++ b/solution.py
@@ -265,7 +265,9 @@
         start(y_copies(s, 1, zl))
         start(y_copies(s, 2, zr))
         x_send(s, (1, 2))
-        give(s, jyz(s, c), (1, 2))
+        block = blk(jyz(s, c), z, ylo)
+        for zz in (zr, zl):
+            rcopy(block, block, gz[s], gd[s] + 1, dev(x, y, zz, 1 - c)).start()
 
     def wave3(s):
         got(rows_of(80), gz[s] + 2)
@@ -310,9 +312,9 @@
         pl.when(c == 0)(lambda: sent(sibw.at[0:4], swaps))
         pl.when(c == 1)(lambda: sent(sibw, swaps))
         for s in range(3):
-            sent(rows_of(240), gz[s])
+            sent(rows_of(400), gz[s])
             sent(rows_of(320), gy[s])
-            sent(rows_of(C), gd[s])
+            sent(rows_of(480), gd[s])
         for s in range(2):
 
             def body(s=s):
@@ -506,6 +508,8 @@
                             groups[g][0][place(kw, g, s % 2, s // 2, half * 4 + d)] = res[
                                 low : low + 16, kh * C + first : kh * C + end
                             ]
+            for one in parts[kw].lanes:
+                one.swaps[half].start()
 
     def add(out, terms):
         val = functools.reduce(lambda a, b: a + b, [t[...].astype(F32) for t in terms])
@@ -531,7 +535,15 @@
             self.buf = wg.at[kw, c]
             send, self.recv = send_sems[g], alloc.take(5)
             self.two = wg.at[kw, 0, 0:2]
-            self.swap = rcopy(wg.at[kw, 1 - c], self.rxs, send, self.recv, sibling)
+            self.swaps = []
+            for half in range(2):
+                part = [slice(None)] * 3
+                part[self.axes.index("z")] = slice(2 * half, 2 * half + 2)
+                self.swaps.append(
+                    rcopy(
+                        wg.at[(kw, 1 - c, *part)], self.rxs.at[tuple(part)], send, self.recv, sibling
+                    )
+                )
             axis = self.axes[0]
             self.me = [here[a] for a in self.axes]
             far_, up, down = ((self.me[0] + k) % 4 for k in (2, 1, 3))
@@ -609,10 +621,7 @@
 
         def step(self, n):
             kw = self.kw
-            if n == 0:
-                for one in self.lanes:
-                    one.swap.start()
-            elif n == 2:
+            if n == 2:
                 for one in self.lanes:
                     one.middle()
             elif n == 3:
@@ -645,7 +654,6 @@
 
     parts = [Reduce(kw) for kw in range(3)]
     weight_part(0)
-    parts[0].step(0)
 
     ex_l1.wait()
     tweight = 1.0 / (1.0 + jnp.full((8, 128), ts[0], jnp.int32).astype(F32) / 250.0)
@@ -659,7 +667,6 @@
     ex_l2 = Exchange(l2, dp, NDP, to_dp)
     ex_l2.send()
     weight_part(1)
-    parts[1].step(0)
     ex_l2.wait()
     sums2 = ex_l2.total()
     denom = jnp.maximum(sums2[1:2], 1.0)
@@ -680,7 +687,6 @@
 
     parts[0].join(coef, sib_coef)
     weight_part(2)
-    parts[2].step(0)
     parts[1].join(coef, sib_coef)
     parts[0].step(2)
 

time: 98.6 us -> 101 us (1.024)
  Pallas kernels: 93.4 us -> 95.9 us
    pallas_call x1, Pallas kernels: 93.4 us -> 95.9 us  [shards(): pl.pallas_call(kernel, out_shape=(pltpu.VMEM((ROWS, COLS, C), BF16), pltp...]
where the time goes in v3:
time: 101 us
  Pallas kernels  95.9 us (95%)
  local copies, waits for them, and re-layouts  3.11 us (3%)
  between operations  1.94 us (2%)
    pallas_call x1, Pallas kernels, shards(): pl.pallas_call(kernel, out_shape=(pltpu.VMEM((ROWS, COLS, C), BF16), pltp...  95.9 us

profile of v3, /device:TPU:1, one launch (start us, length us, event | category | flops | bytes accessed | tf_op | source)
XLA Modules:
  0.0 101.0 jit_solution(1841683758234675836)
XLA Ops:
  1.9 95.9 %shard_map.136 = (bf16[16,64,640]{2,1,0:T(8,128)(2,1)S(1)}, f32[9,40,640]{2,1,0:T(8,128)S(1)}, f32[8,640]{1,0:T(8,128)S(1)}) custom-call(s32[1]{0:T(128)S(6)} %copy.19.ts, s32[1]{0:T(128)S(6)} %copy.20.bk, s32[4]{0:T(128)} %clip.1, bf16[16,64,640]{2,1,0:T(8,128)(2,1)} %bitcast.13, bf16[16,64,640]{2,1,0:T(8,128)(2,1)} %bitcast.14, ...), custom_call_target="tpu_custom_call" | custom-call | flops 22649241600 | bytes 8388608 | tf_op jit(solution)/shard_map/pallas_call | solution.py:785
  97.8 0.6 slice_reduce_fusion
  98.5 0.5 slice_bitcast_fusion
  99.0 1.1 %copy.17 = bf16[1,16,64,640]{3,2,1,0:T(8,128)(2,1)} copy(bf16[1,16,64,640]{3,2,1,0:T(8,128)(2,1)S(1)} %bitcast.11) | data formatting | bytes 2621440
  100.0 0.9 copy.18

commit v4 on v1

--- a/solution.py
+++ b/solution.py
@@ -409,23 +409,26 @@
             out = pl.ds(pl.multiple_of(m * 512, 512), 512)
             acc[out, :] = part if fresh else acc[out, :] + part
 
-    activate(0, 8)
+    activate(0, 4)
     wave2(1)
+    activate(4, 8)
     wave3(0)
-    activate(8, ROWS)
+    activate(8, 12)
     wave3(1)
+    activate(12, ROWS)
     wave4(0)
     wave_x(0, (1, 2))
     turn(0, 3)
     wave2(2)
     wave_x(0, (3,))
+    turn(3, 6)
+    wave4(1)
+    wave_x(1, (1, 2, 3))
     from_sibling(0)
     forward(2 * odd, 2, True)
-    wave4(1)
-    wave_x(1, (1, 2, 3))
     wave3(2)
     wave_x(0, (4, 5, 6, 7))
-    turn(3, 8)
+    turn(6, 8)
     from_sibling_x(0)
     forward(2 - 2 * odd, 2)
     wave_x(1, (4, 5, 6, 7))
@@ -458,7 +461,8 @@
     rcopy(es.at[1], er.at[1], esem, esem + 1, left).start()
 
     def back(m):
-        low = m * (PADPIX // 3)
+        rows = PADPIX // 4
+        low = m * rows
         w = jnp.concatenate(
             [
                 jnp.concatenate([wg_all[3 * kh + kw] for kw in (2, 1, 0)], axis=1)
@@ -467,10 +471,10 @@
             axis=0,
         )
         part = lax.dot_general(
-            e3[COLS + low : COLS + low + PADPIX // 3, :], w, NT, preferred_element_type=F32
+            e3[COLS + low : COLS + low + rows, :], w, NT, preferred_element_type=F32
         )
         for kh in range(3):
-            out = slice(low + kh * COLS, low + kh * COLS + PADPIX // 3)
+            out = slice(low + kh * COLS, low + kh * COLS + rows)
             dacc[out, :] = dacc[out, :] + part[:, kh * C : (kh + 1) * C]
 
     NRED = 9
@@ -706,6 +710,10 @@
     parts[2].step(4)
     parts[1].step(5)
     parts[0].step(6)
+    back(3)
+    parts[2].step(5)
+    parts[1].step(6)
+    parts[0].step(7)
 
     def through(r, carry):
         a, b = carry
@@ -723,9 +731,9 @@
     )
     ex_g1 = Exchange(g1, lon, NLON, to_lon)
     ex_g1.send()
-    parts[2].step(5)
-    parts[1].step(6)
-    parts[0].step(7)
+    parts[2].step(6)
+    parts[1].step(7)
+    parts[0].step(8)
     ex_g1.wait()
     pan = ex_g1.total()
     g2[dp] = pan
@@ -734,22 +742,20 @@
     means = group_sum(pan * gain) / COUNT
     m1, m2 = means[0:1], means[1:2]
 
-    @pl.loop(0, ROWS)
-    def _(r):
+    def input_gradient(r):
         normed = (lat[r].astype(F32) - mean) * rstd
         dn = dacc[at_row(r + 2), :] * gain
         g = e3[at_row(r + 2), C : 2 * C].astype(F32) * coef
         igrad[r] = (g + rstd * (dn - m1 - normed * m2)).astype(BF16)
 
-    parts[2].step(6)
-    parts[1].step(7)
-    parts[0].step(8)
+    pl.loop(0, 8)(input_gradient)
+    parts[2].step(7)
+    parts[1].step(8)
+    pl.loop(8, ROWS)(input_gradient)
     ex_g2.wait()
     totals = ex_g2.total() * SCALE
     wide = jnp.concatenate([losses] + [jnp.zeros_like(losses)] * 4, axis=1)
     sg_out[...] = jnp.where(sub == 3, wide, totals)
-    parts[2].step(7)
-    parts[1].step(8)
     parts[2].step(8)
     reduce_sends_done()
     assert alloc.used <= NUM_SEMS, alloc.used

time: 98.6 us -> 101 us (1.024)
  Pallas kernels: 93.4 us -> 95.4 us
    pallas_call x1, Pallas kernels: 93.4 us -> 95.4 us  [shards(): pl.pallas_call(kernel, out_shape=(pltpu.VMEM((ROWS, COLS, C), BF16), pltp...]
where the time goes in v4:
time: 101 us; the launch traced here: 100 us
  Pallas kernels  95.4 us (94%)
  local copies, waits for them, and re-layouts  3.11 us (3%)
  between operations  1.94 us (2%)
    pallas_call x1, Pallas kernels, shards(): pl.pallas_call(kernel, out_shape=(pltpu.VMEM((ROWS, COLS, C), BF16), pltp...  95.4 us

profile of v4, /device:TPU:1, one launch (start us, length us, event | category | flops | bytes accessed | tf_op | source)
XLA Modules:
  0.0 100.5 jit_solution(7844303371110161440)
XLA Ops:
  1.9 95.4 %shard_map.136 = (bf16[16,64,640]{2,1,0:T(8,128)(2,1)S(1)}, f32[9,40,640]{2,1,0:T(8,128)S(1)}, f32[8,640]{1,0:T(8,128)S(1)}) custom-call(s32[1]{0:T(128)S(6)} %copy.19.ts, s32[1]{0:T(128)S(6)} %copy.20.bk, s32[4]{0:T(128)} %clip.1, bf16[16,64,640]{2,1,0:T(8,128)(2,1)} %bitcast.13, bf16[16,64,640]{2,1,0:T(8,128)(2,1)} %bitcast.14, ...), custom_call_target="tpu_custom_call" | custom-call | flops 22649241600 | bytes 8388608 | tf_op jit(solution)/shard_map/pallas_call | solution.py:785
  97.4 0.6 slice_reduce_fusion
  98.0 0.5 slice_bitcast_fusion
  98.5 1.1 %copy.17 = bf16[1,16,64,640]{3,2,1,0:T(8,128)(2,1)} copy(bf16[1,16,64,640]{3,2,1,0:T(8,128)(2,1)S(1)} %bitcast.11) | data formatting | bytes 2621440
  99.6 0.9 copy.18

commit v5 on v1

--- a/solution.py
+++ b/solution.py
@@ -397,17 +397,14 @@
             ).astype(BF16)
 
     def forward(tap, count, fresh=False):
-        @pl.loop(0, 2)
-        def _(m):
-            fields = []
-            for n in range(count):
-                kh, kw = (tap + n) // 3, (tap + n) % 3
-                rows = pl.ds(pl.multiple_of(kh * COLS + m * 512, COLS), 512)
-                fields.append(x3[rows, pl.ds(pl.multiple_of(kw * C, 128), C)])
-            w = wg_all[pl.ds(tap, count)].reshape(count * C, C)
-            part = jnp.dot(jnp.concatenate(fields, axis=1), w, preferred_element_type=F32)
-            out = pl.ds(pl.multiple_of(m * 512, 512), 512)
-            acc[out, :] = part if fresh else acc[out, :] + part
+        fields = []
+        for n in range(count):
+            kh, kw = (tap + n) // 3, (tap + n) % 3
+            rows = pl.ds(pl.multiple_of(kh * COLS, COLS), PIX)
+            fields.append(x3[rows, pl.ds(pl.multiple_of(kw * C, 128), C)])
+        w = wg_all[pl.ds(tap, count)].reshape(count * C, C)
+        part = jnp.dot(jnp.concatenate(fields, axis=1), w, preferred_element_type=F32)
+        acc[...] = part if fresh else acc[...] + part
 
     activate(0, 8)
     wave2(1)
@@ -458,7 +455,8 @@
     rcopy(es.at[1], er.at[1], esem, esem + 1, left).start()
 
     def back(m):
-        low = m * (PADPIX // 3)
+        rows = PADPIX // 2
+        low = m * rows
         w = jnp.concatenate(
             [
                 jnp.concatenate([wg_all[3 * kh + kw] for kw in (2, 1, 0)], axis=1)
@@ -467,10 +465,10 @@
             axis=0,
         )
         part = lax.dot_general(
-            e3[COLS + low : COLS + low + PADPIX // 3, :], w, NT, preferred_element_type=F32
+            e3[COLS + low : COLS + low + rows, :], w, NT, preferred_element_type=F32
         )
         for kh in range(3):
-            out = slice(low + kh * COLS, low + kh * COLS + PADPIX // 3)
+            out = slice(low + kh * COLS, low + kh * COLS + rows)
             dacc[out, :] = dacc[out, :] + part[:, kh * C : (kh + 1) * C]
 
     NRED = 9
@@ -492,20 +490,18 @@
         err = jnp.concatenate(
             [e3[(2 - kh) * COLS : (2 - kh) * COLS + PADPIX, C : 2 * C] for kh in range(3)], axis=1
         )
-        for half in range(2):
-            top = kw * C + half * (C // 2)
-            res = jnp.dot(x3t[top : top + C // 2, :], err, preferred_element_type=F32)
-            res = res.astype(BF16)
-            for d in range(4):
-                for t in range(5):
-                    low = d * 80 + t * 16
-                    for kh in range(3):
-                        s = kh * 5 + t
-                        for g in range(3):
-                            first, end = LANES[g]
-                            groups[g][0][place(kw, g, s % 2, s // 2, half * 4 + d)] = res[
-                                low : low + 16, kh * C + first : kh * C + end
-                            ]
+        res = jnp.dot(x3t[kw * C : (kw + 1) * C, :], err, preferred_element_type=F32)
+        res = res.astype(BF16)
+        for d in range(8):
+            for t in range(5):
+                low = d * 80 + t * 16
+                for kh in range(3):
+                    s = kh * 5 + t
+                    for g in range(3):
+                        first, end = LANES[g]
+                        groups[g][0][place(kw, g, s % 2, s // 2, d)] = res[
+                            low : low + 16, kh * C + first : kh * C + end
+                        ]
 
     def add(out, terms):
         val = functools.reduce(lambda a, b: a + b, [t[...].astype(F32) for t in terms])
@@ -686,26 +682,23 @@
 
     sent(es, esem)
     got(er, esem + 1)
+    parts[2].join(coef, sib_coef)
 
     @pl.loop(0, ROWS)
     def _(r):
         put_sides(e3, r + 2, e3[at_row(r + 2), C : 2 * C].astype(F32), er, r)
 
     parts[1].step(2)
-    parts[2].join(coef, sib_coef)
     parts[0].step(3)
+    parts[2].step(2)
     back(0)
-    parts[2].step(2)
     parts[1].step(3)
     parts[0].step(4)
+    parts[2].step(3)
     back(1)
-    parts[2].step(3)
     parts[1].step(4)
     parts[0].step(5)
-    back(2)
     parts[2].step(4)
-    parts[1].step(5)
-    parts[0].step(6)
 
     def through(r, carry):
         a, b = carry
@@ -723,9 +716,9 @@
     )
     ex_g1 = Exchange(g1, lon, NLON, to_lon)
     ex_g1.send()
+    parts[1].step(5)
+    parts[0].step(6)
     parts[2].step(5)
-    parts[1].step(6)
-    parts[0].step(7)
     ex_g1.wait()
     pan = ex_g1.total()
     g2[dp] = pan
@@ -734,21 +727,24 @@
     means = group_sum(pan * gain) / COUNT
     m1, m2 = means[0:1], means[1:2]
 
-    @pl.loop(0, ROWS)
-    def _(r):
+    def input_gradient(r):
         normed = (lat[r].astype(F32) - mean) * rstd
         dn = dacc[at_row(r + 2), :] * gain
         g = e3[at_row(r + 2), C : 2 * C].astype(F32) * coef
         igrad[r] = (g + rstd * (dn - m1 - normed * m2)).astype(BF16)
 
+    pl.loop(0, 8)(input_gradient)
     parts[2].step(6)
+    parts[1].step(6)
+    parts[0].step(7)
+    pl.loop(8, ROWS)(input_gradient)
+    parts[2].step(7)
     parts[1].step(7)
     parts[0].step(8)
     ex_g2.wait()
     totals = ex_g2.total() * SCALE
     wide = jnp.concatenate([losses] + [jnp.zeros_like(losses)] * 4, axis=1)
     sg_out[...] = jnp.where(sub == 3, wide, totals)
-    parts[2].step(7)
     parts[1].step(8)
     parts[2].step(8)
     reduce_sends_done()

time: 98.6 us -> 98.4 us (level)
  no operation moved by 1% of the time
where the time goes in v5:
time: 98.4 us; the launch traced here: 98.3 us
  Pallas kernels  93.2 us (95%)
  local copies, waits for them, and re-layouts  3.11 us (3%)
  between operations  1.94 us (2%)
    pallas_call x1, Pallas kernels, shards(): pl.pallas_call(kernel, out_shape=(pltpu.VMEM((ROWS, COLS, C), BF16), pltp...  93.2 us
    unnamed x2, local copies, waits for them, and re-layouts  1.98 us

profile of v5, /device:TPU:1, one launch (start us, length us, event | category | flops | bytes accessed | tf_op | source)
XLA Modules:
  0.0 98.3 jit_solution(3200477449875231156)
XLA Ops:
  1.9 93.2 %shard_map.136 = (bf16[16,64,640]{2,1,0:T(8,128)(2,1)S(1)}, f32[9,40,640]{2,1,0:T(8,128)S(1)}, f32[8,640]{1,0:T(8,128)S(1)}) custom-call(s32[1]{0:T(128)S(6)} %copy.19.ts, s32[1]{0:T(128)S(6)} %copy.20.bk, s32[4]{0:T(128)} %clip.1, bf16[16,64,640]{2,1,0:T(8,128)(2,1)} %bitcast.13, bf16[16,64,640]{2,1,0:T(8,128)(2,1)} %bitcast.14, ...), custom_call_target="tpu_custom_call" | custom-call | flops 22649241600 | bytes 8388608 | tf_op jit(solution)/shard_map/pallas_call | solution.py:775
  95.1 0.6 slice_reduce_fusion
  95.8 0.5 slice_bitcast_fusion
  96.3 1.1 %copy.17 = bf16[1,16,64,640]{3,2,1,0:T(8,128)(2,1)} copy(bf16[1,16,64,640]{3,2,1,0:T(8,128)(2,1)S(1)} %bitcast.11) | data formatting | bytes 2621440
  97.3 0.9 copy.18

commit v6 on v5

--- a/solution.py
+++ b/solution.py
@@ -397,14 +397,17 @@
             ).astype(BF16)
 
     def forward(tap, count, fresh=False):
-        fields = []
-        for n in range(count):
-            kh, kw = (tap + n) // 3, (tap + n) % 3
-            rows = pl.ds(pl.multiple_of(kh * COLS, COLS), PIX)
-            fields.append(x3[rows, pl.ds(pl.multiple_of(kw * C, 128), C)])
-        w = wg_all[pl.ds(tap, count)].reshape(count * C, C)
-        part = jnp.dot(jnp.concatenate(fields, axis=1), w, preferred_element_type=F32)
-        acc[...] = part if fresh else acc[...] + part
+        @pl.loop(0, 2)
+        def _(m):
+            fields = []
+            for n in range(count):
+                kh, kw = (tap + n) // 3, (tap + n) % 3
+                rows = pl.ds(pl.multiple_of(kh * COLS + m * 512, COLS), 512)
+                fields.append(x3[rows, pl.ds(pl.multiple_of(kw * C, 128), C)])
+            w = wg_all[pl.ds(tap, count)].reshape(count * C, C)
+            part = jnp.dot(jnp.concatenate(fields, axis=1), w, preferred_element_type=F32)
+            out = pl.ds(pl.multiple_of(m * 512, 512), 512)
+            acc[out, :] = part if fresh else acc[out, :] + part
 
     activate(0, 8)
     wave2(1)
@@ -692,13 +695,13 @@
     parts[0].step(3)
     parts[2].step(2)
     back(0)
+    parts[2].step(3)
     parts[1].step(3)
     parts[0].step(4)
-    parts[2].step(3)
     back(1)
+    parts[2].step(4)
     parts[1].step(4)
     parts[0].step(5)
-    parts[2].step(4)
 
     def through(r, carry):
         a, b = carry
@@ -716,9 +719,9 @@
     )
     ex_g1 = Exchange(g1, lon, NLON, to_lon)
     ex_g1.send()
+    parts[2].step(5)
     parts[1].step(5)
     parts[0].step(6)
-    parts[2].step(5)
     ex_g1.wait()
     pan = ex_g1.total()
     g2[dp] = pan

time: 98.4 us -> 96.1 us (0.977)
  Pallas kernels: 93.2 us -> 90.9 us
    pallas_call x1, Pallas kernels: 93.2 us -> 90.9 us  [shards(): pl.pallas_call(kernel, out_shape=(pltpu.VMEM((ROWS, COLS, C), BF16), pltp...]
where the time goes in v6:
time: 96.1 us; the launch traced here: 95.9 us
  Pallas kernels  90.9 us (95%)
  local copies, waits for them, and re-layouts  3.11 us (3%)
  between operations  1.94 us (2%)
    pallas_call x1, Pallas kernels, shards(): pl.pallas_call(kernel, out_shape=(pltpu.VMEM((ROWS, COLS, C), BF16), pltp...  90.9 us
    unnamed x2, local copies, waits for them, and re-layouts  1.98 us

profile of v6, /device:TPU:1, one launch (start us, length us, event | category | flops | bytes accessed | tf_op | source)
XLA Modules:
  0.0 95.9 jit_solution(11081750077220370612)
XLA Ops:
  1.9 90.9 %shard_map.136 = (bf16[16,64,640]{2,1,0:T(8,128)(2,1)S(1)}, f32[9,40,640]{2,1,0:T(8,128)S(1)}, f32[8,640]{1,0:T(8,128)S(1)}) custom-call(s32[1]{0:T(128)S(6)} %copy.19.ts, s32[1]{0:T(128)S(6)} %copy.20.bk, s32[4]{0:T(128)} %clip.1, bf16[16,64,640]{2,1,0:T(8,128)(2,1)} %bitcast.13, bf16[16,64,640]{2,1,0:T(8,128)(2,1)} %bitcast.14, ...), custom_call_target="tpu_custom_call" | custom-call | flops 22649241600 | bytes 8388608 | tf_op jit(solution)/shard_map/pallas_call | solution.py:778
  92.8 0.6 slice_reduce_fusion
  93.5 0.5 slice_bitcast_fusion
  94.0 1.1 %copy.17 = bf16[1,16,64,640]{3,2,1,0:T(8,128)(2,1)} copy(bf16[1,16,64,640]{3,2,1,0:T(8,128)(2,1)S(1)} %bitcast.11) | data formatting | bytes 2621440
  95.0 0.9 copy.18
